TPU v7x, 512 devices: a whole 4x4x16 slice. The times are simulated.
512 devices in a mesh: row: 32 (over y, z_lo, core), col: 16 (over z_hi, x).
Axes of the slice: x: 4, y: 4, z: 16 (z_hi: 4, z_lo: 4; z = z_hi * 4 + z_lo), core: 2. Of those that a mesh axis runs over, the one named last changes fastest.
Arguments:
- queries: bfloat16 [32768, 2048], P('row', 'col'), may hold values from -122 to 122
- key_vectors: bfloat16 [32768, 128], P(('col', 'row')), may hold values from -6.1 to 6.1
- value_vectors: bfloat16 [32768, 128], P(('col', 'row')), may hold values from -6 to 6
- block_mask: int32 [64, 64], replicated, may hold values from 0 to 1, as said below
Outputs:
- attended: bfloat16 [32768, 2048], P('row', 'col')
Inputs may be any that keep to these rules, and one draw needn't show every extreme that they name: `block_mask`: query block i attends to key block j only when j <= i; every block attends to itself; a tile (r, c) lists at most 3 pairs, and the tiles that hold the diagonal list exactly 3.
All inputs are finite; a program needn't handle non-finite values.
Results may differ from a plain program's by a relative error of at most 0.015.
Values may be sent and summed in bfloat16 or wider, within the bound.
A program may use at most 192 MiB of HBM per device.

v0:
```python
import jax
import jax.numpy as jnp
from jax import lax
from jax.sharding import PartitionSpec as P

HEAD_DIM = 128
BLOCK = 512
SLOTS = 3


NEG_FILL = -1e30


def tile_terms(queries, key_stretch, value_stretch, tile_flags, row_start, key_start):
    row_count = queries.shape[0]
    head_width = key_stretch.shape[1]
    head_count = queries.shape[1] // head_width
    q_blocks = tile_flags.shape[0]
    k_blocks = tile_flags.shape[1]
    block_len = row_count // q_blocks
    pair_count = q_blocks * k_blocks
    score_scale = head_width ** (-0.5)
    running = jnp.cumsum(tile_flags.reshape(pair_count))
    shaped = queries.reshape(row_count, head_count, head_width)
    group_size = min(head_count, 4)
    maxima = jnp.full((head_count, row_count), NEG_FILL, jnp.float32)
    totals = jnp.zeros((head_count, row_count), jnp.float32)
    accumulated = jnp.zeros((row_count, head_count, head_width), jnp.float32)
    for slot_index in range(SLOTS):
        position = jnp.minimum(jnp.sum((running <= slot_index).astype(jnp.int32)), pair_count - 1)
        active = running[pair_count - 1] > slot_index
        qstart = position // k_blocks * block_len
        kstart = position % k_blocks * block_len
        kblock = lax.dynamic_slice_in_dim(key_stretch, kstart, block_len, 0)
        vblock = lax.dynamic_slice_in_dim(value_stretch, kstart, block_len, 0)
        query_pos = row_start + qstart + jnp.arange(block_len, dtype=jnp.int32)
        key_pos = key_start + kstart + jnp.arange(block_len, dtype=jnp.int32)
        allowed = jnp.logical_and(key_pos[None, :] <= query_pos[:, None], active)
        for head_first in range(0, head_count, group_size):
            query_part = lax.dynamic_slice_in_dim(
                shaped[:, head_first : head_first + group_size], qstart, block_len, 0
            )
            scores = (
                jnp.einsum("qhd,kd->hqk", query_part, kblock, preferred_element_type=jnp.float32)
                * score_scale
            )
            scores = jnp.where(allowed[None], scores, NEG_FILL)
            start_pair = (jnp.int32(head_first), qstart)
            old_max = lax.dynamic_slice(maxima, start_pair, (group_size, block_len))
            new_max = jnp.maximum(old_max, jnp.max(scores, axis=-1))
            factor = jnp.exp(old_max - new_max)
            unnormed = jnp.where(allowed[None], jnp.exp(scores - new_max[:, :, None]), 0.0)
            old_tot = lax.dynamic_slice(totals, start_pair, (group_size, block_len))
            new_tot = old_tot * factor + jnp.sum(unnormed, axis=-1)
            weights = unnormed.astype(jnp.bfloat16)
            mixed_values = jnp.einsum(
                "hqk,kd->qhd", weights, vblock, preferred_element_type=jnp.float32
            )
            acc_start = (qstart, jnp.int32(head_first), jnp.int32(0))
            old_acc = lax.dynamic_slice(accumulated, acc_start, (block_len, group_size, head_width))
            new_acc = old_acc * factor.T[:, :, None] + mixed_values
            maxima = lax.dynamic_update_slice(maxima, new_max, start_pair)
            totals = lax.dynamic_update_slice(totals, new_tot, start_pair)
            accumulated = lax.dynamic_update_slice(accumulated, new_acc, acc_start)
    return (maxima, totals, accumulated)


def body(queries, key_vectors, value_vectors, block_mask):
    row_index = lax.axis_index("row")
    col_index = lax.axis_index("col")
    gathered_q = lax.all_gather(queries, "col", axis=1, tiled=True)
    key_stretch, value_stretch = (
        lax.all_gather(key_vectors, "row", axis=0, tiled=True),
        lax.all_gather(value_vectors, "row", axis=0, tiled=True),
    )
    row_count = gathered_q.shape[0]
    stretch_len = key_stretch.shape[0]
    q_blocks = row_count // BLOCK
    k_blocks = stretch_len // BLOCK
    head_count = gathered_q.shape[1] // HEAD_DIM
    tile_flags = lax.dynamic_slice(
        block_mask, (row_index * q_blocks, col_index * k_blocks), (q_blocks, k_blocks)
    )
    maxima, totals, accumulated = tile_terms(
        gathered_q,
        key_stretch,
        value_stretch,
        tile_flags,
        row_index * row_count,
        col_index * stretch_len,
    )
    global_max = lax.pmax(maxima.astype(jnp.bfloat16), "col").astype(maxima.dtype)
    weight = jnp.exp(maxima - global_max)
    denominator = lax.psum((totals * weight).astype(jnp.bfloat16), "col").astype(jnp.float32)
    shares_bf = (
        (accumulated * weight.T[:, :, None])
        .reshape(row_count, head_count * HEAD_DIM)
        .astype(jnp.bfloat16)
    )
    col_count = lax.axis_size("col")
    feature_width = queries.shape[1]
    received = lax.all_to_all(shares_bf, "col", split_axis=1, concat_axis=0, tiled=True)
    numerator = jnp.sum(
        received.reshape(col_count, row_count, feature_width).astype(jnp.float32), axis=0
    )
    feature_heads = (
        col_index * feature_width + jnp.arange(feature_width, dtype=jnp.int32)
    ) // HEAD_DIM
    head_select = (
        jnp.arange(head_count, dtype=jnp.int32)[:, None] == feature_heads[None, :]
    ).astype(jnp.float32)
    spread_den = jnp.dot(denominator.T, head_select, precision=lax.Precision.HIGHEST)
    return (numerator / spread_den).astype(jnp.bfloat16)


def solution(mesh):
    placed = (P("row", "col"), P(("col", "row"), None), P(("col", "row"), None), P())
    return jax.shard_map(
        body, mesh=mesh, in_specs=placed, out_specs=P("row", "col"), check_vma=False
    )
```

profile of v0, /device:TPU:24, one launch (start us, length us, event | category | flops | bytes accessed | tf_op | source)
XLA Modules:
  0.0 605.6 jit_solution(8943659033357488301)
XLA Ops:
  6.5 1.8 copy.36
  8.4 0.8 dynamic_slice.164
  9.4 0.7 fusion.299
  15.4 47.4 %all_gather.9 = bf16[2048,128]{1,0:T(8,128)(2,1)S(1)} all-gather(bf16[64,128]{1,0:T(8,128)(2,1)} %param.5), channel_id=1, replica_groups=mesh['row'=32,'col'=16] {'row'}, dimensions={0}, use_global_device_ids=true | all-gather | bytes 540672 | tf_op jit(solution)/shard_map/all_gather | solution.py:73
  62.8 90.8 %all_gather.11 = bf16[2048,128]{1,0:T(8,128)(2,1)S(1)} all-gather(bf16[64,128]{1,0:T(8,128)(2,1)} %param.6), channel_id=1, replica_groups=mesh['row'=32,'col'=16] {'row'}, dimensions={0}, use_global_device_ids=true | all-gather | bytes 540672 | tf_op jit(solution)/shard_map/all_gather | solution.py:74
  153.7 2.7 fusion.338
  156.3 2.6 fusion.203
  159.7 0.7 fusion.195
  161.1 0.7 fusion.199
  161.8 0.7 fusion.191
  162.6 0.7 fusion.187
  163.3 0.7 fusion.185
  164.0 0.7 fusion.183
  164.9 8.2 %fusion.3 = (f32[4,512]{1,0:T(4,128)S(1)}, f32[4,512]{1,0:T(4,128)S(1)}, f32[4,512]{1,0:T(4,128)S(1)}, f32[4,512]{1,0:T(4,128)S(1)}, f32[512,512,4]{1,0,2:T(8,128)}) fusion(pred[512,512]{0,1:T(8,128)(4,1)S(1)} %compare_and_fusion.2, f32[512,512,4]{1,0,2:T(8,128)S(1)} %fusion.201, f32[512,512,4]{1,0,2:T(8,128)S(1)} %fusion.199, f32[512,512,4]{1,0,2:T(8,128)} %fusion.203, ...), kind=kOutput, calls=%fused_computation.29 | convolution fusion | flops 281010176 | bytes 17727496 | tf_op jit(solution)/shard_map/qhd,kd->hqk/dot_general | solution.py:44
  174.5 4.7 fusion.7
  179.5 4.7 fusion.11
  184.4 92.6 %pmax.7 = bf16[16,1024]{1,0:T(8,128)(2,1)S(1)} all-reduce(bf16[16,1024]{1,0:T(8,128)(2,1)S(1)} %convert_element_type.85), channel_id=1, replica_groups=mesh['row'=32,'col'=16] {'col'}, use_global_device_ids=true, to_apply=%region_16.17 | all-reduce | flops 16384 | bytes 65536 | tf_op jit(solution)/shard_map/pmax | solution.py:92
  277.0 7.9 %fusion.18 = (f32[4,512]{1,0:T(4,128)S(1)}, f32[4,512]{1,0:T(4,128)S(1)}, f32[4,512]{1,0:T(4,128)S(1)}, f32[4,512]{1,0:T(4,128)S(1)}) fusion(f32[512,512,4]{1,0,2:T(8,128)} %get-tuple-element.86, f32[4,512]{1,0:T(4,128)S(1)} %get-tuple-element.49, pred[512,512]{0,1:T(8,128)(4,1)S(1)} %compare_and_fusion.2, f32[4,512]{1,0:T(4,128)} %get-tuple-element.85, ...), kind=kLoop, calls=%fused_computation.44 | loop fusion | flops 20963328 | bytes 17104896 | tf_op jit(solution)/shard_map/reduce_sum | solution.py:54
  284.9 0.8 add_dynamic-update-slice_fusion.8
  285.8 1.1 broadcast_in_dim.176
  286.8 1.1 copy-done.16
  287.9 1.3 fusion.177
  289.2 0.9 copy-done.15
  290.1 1.3 fusion.171
  291.5 0.9 copy-done.13
  292.3 1.3 fusion.165
  293.8 1.3 fusion.159
  295.1 1.1 copy-done.18
  296.2 1.2 copy-done.7
  297.4 1.2 copy-done.9
  298.6 4.2 fusion.26
  302.9 1.3 fusion.153
  304.3 1.3 fusion.147
  305.6 1.3 fusion.141
  307.0 1.3 fusion.135
  308.4 0.7 copy-done.17
  309.1 1.4 copy-done.1
  310.5 1.2 copy-done.3
  311.7 4.3 fusion.34
  316.0 1.3 fusion.129
  317.4 1.3 fusion.123
  318.7 1.3 fusion.117
  320.1 1.3 fusion.111
  321.5 3.3 multiply_convert_fusion
  324.8 10.0 %all-to-all-start = ((bf16[1024,16,128]{0,2,1:T(8,128)(2,1)}), bf16[1024,16,128]{0,2,1:T(8,128)(2,1)}, u32[]{:S(2)}, u32[]{:S(2)}) async-start(bf16[1024,16,128]{0,2,1:T(8,128)(2,1)} %multiply_convert_fusion), calls=%async_computation | async-start | bytes 8388608 | tf_op jit(solution)/shard_map/all_to_all | solution.py:102
  334.9 259.2 %psum.7 = bf16[16,1024]{1,0:T(8,128)(2,1)S(1)} all-reduce(bf16[16,1024]{1,0:T(8,128)(2,1)S(1)} %get-tuple-element.58), channel_id=1, replica_groups=mesh['row'=32,'col'=16] {'col'}, use_global_device_ids=true, to_apply=%region_30.31 | all-reduce | flops 16384 | bytes 65536 | tf_op jit(solution)/shard_map/psum | solution.py:94
  594.0 3.2 convert_reduce_fusion
  597.4 1.0 fusion.180
  (96 shorter events, 6.0 us)
Async XLA Ops:
  6.5 147.1 %all-gather.2.cloned.1.call-start = ((), (), s32[]{:S(2)}) async-start(), calls=%async_computation.1 | async-start | bytes 4456448 | tf_op jit(solution)/shard_map/all_gather | solution.py:71
  159.7 5.0 copy-start.14
  160.4 14.1 %copy-start.10 = (f32[512,512,4]{1,0,2:T(8,128)}, f32[512,512,4]{1,0,2:T(8,128)S(1)}, u32[]{:S(2)}) copy-start(f32[512,512,4]{1,0,2:T(8,128)S(1)} %fusion.195) | copy-start | bytes 12582916
  161.1 13.4 %copy-start.8 = (f32[512,512,4]{1,0,2:T(8,128)}, f32[512,512,4]{1,0,2:T(8,128)S(1)}, u32[]{:S(2)}) copy-start(f32[512,512,4]{1,0,2:T(8,128)S(1)} %fusion.193) | copy-start | bytes 12582916
  161.8 3.0 copy-start.12
  162.5 12.0 %copy-start.6 = (f32[512,512,4]{1,0,2:T(8,128)}, f32[512,512,4]{1,0,2:T(8,128)S(1)}, u32[]{:S(2)}) copy-start(f32[512,512,4]{1,0,2:T(8,128)S(1)} %fusion.191) | copy-start | bytes 12582916
  163.3 16.2 %copy-start.4 = (f32[512,512,4]{1,0,2:T(8,128)}, f32[512,512,4]{1,0,2:T(8,128)S(1)}, u32[]{:S(2)}) copy-start(f32[512,512,4]{1,0,2:T(8,128)S(1)} %fusion.187) | copy-start | bytes 12582916
  164.0 15.5 %copy-start.2 = (f32[512,512,4]{1,0,2:T(8,128)}, f32[512,512,4]{1,0,2:T(8,128)S(1)}, u32[]{:S(2)}) copy-start(f32[512,512,4]{1,0,2:T(8,128)S(1)} %fusion.185) | copy-start | bytes 12582916
  164.7 14.8 %copy-start = (f32[512,512,4]{1,0,2:T(8,128)}, f32[512,512,4]{1,0,2:T(8,128)S(1)}, u32[]{:S(2)}) copy-start(f32[512,512,4]{1,0,2:T(8,128)S(1)} %fusion.183) | copy-start | bytes 12582916
  173.0 0.6 copy-start.22
  173.7 5.5 copy-start.20
  277.0 7.9 %copy-start.23 = (f32[4,512]{1,0:T(4,128)S(1)}, f32[4,512]{1,0:T(4,128)}, u32[]{:S(2)}) copy-start(f32[4,512]{1,0:T(4,128)} %copy-done.22) | copy-start | bytes 24580
  277.0 8.0 %copy-start.21 = (f32[4,512]{1,0:T(4,128)S(1)}, f32[4,512]{1,0:T(4,128)}, u32[]{:S(2)}) copy-start(f32[4,512]{1,0:T(4,128)} %get-tuple-element.53) | copy-start | bytes 24580
  285.8 2.2 copy-start.16
  285.8 2.2 copy-start.24
  287.9 2.2 copy-start.15
  290.1 2.2 copy-start.13
  290.1 3.6 copy-start.19
  292.3 2.7 copy-start.11
  292.3 3.9 copy-start.18
  293.7 3.6 copy-start.7
  293.8 4.8 copy-start.9
  305.6 2.7 copy-start.5
  305.6 3.5 copy-start.17
  307.0 3.4 copy-start.1
  307.0 4.6 copy-start.3
  324.8 269.2 %all-to-all-start = ((bf16[1024,16,128]{0,2,1:T(8,128)(2,1)}), bf16[1024,16,128]{0,2,1:T(8,128)(2,1)}, u32[]{:S(2)}, u32[]{:S(2)}) async-start(bf16[1024,16,128]{0,2,1:T(8,128)(2,1)} %multiply_convert_fusion), calls=%async_computation | async-start | bytes 8388608 | tf_op jit(solution)/shard_map/all_to_all | solution.py:102
Sparse Core Ops, SparseCore 0:
  10.4 120.1 all-gather.1
where the time goes:
time: 615 us; the launch traced here: 606 us
  blocking collectives  490 us (80%)
  matrix products  42.3 us (7%)
  other arithmetic  27.8 us (5%)
  between operations  18.4 us (3%)
  local copies, waits for them, and re-layouts  17.1 us (3%)
  starting transfers between devices  10 us (2%)
    psum x1, blocking collectives, body(): lax.psum((totals * weight).astype(jnp.bfloat16), 'col').astype(jnp.float32)  259 us
    pmax x1, blocking collectives, body(): lax.pmax(maxima.astype(jnp.bfloat16), 'col').astype(maxima.dtype)  92.6 us
    all_gather x1, blocking collectives, body(): lax.all_gather(value_vectors, 'row', axis=0, tiled=True)  90.8 us
    all_gather x1, blocking collectives, body(): lax.all_gather(key_vectors, 'row', axis=0, tiled=True)  47.4 us
    dot_general x12, matrix products, tile_terms(): jnp.einsum('qhd,kd->hqk', query_part, kblock, preferred_element_type=jnp....  25.8 us
    reduce_sum x3, other arithmetic, tile_terms(): new_tot = old_tot * factor + jnp.sum(unnormed, axis=-1)  16.4 us
    dot_general x12, matrix products, tile_terms(): jnp.einsum('hqk,kd->qhd', weights, vblock, preferred_element_type=jnp.flo...  15.5 us
  transfers between devices with their start and end apart: 2, of which 0 were waited for; matrix products, arithmetic and copies ran while one was open for 1% of the time, Pallas kernels for 0%

commit v1 on v0

v1 whole, which is shorter than its diff:
```python
import jax
import jax.numpy as jnp
from jax import lax
from jax.experimental import pallas as pl
from jax.experimental.pallas import tpu as pltpu
from jax.sharding import PartitionSpec as P

HEAD_DIM = 128
BLOCK = 512
SLOTS = 3
RING = 4
ZRING = 16
NSLOT = SLOTS * RING
PIECE = 128
HALF = 64
SUMROWS = 16
NEG_FILL = -1e30
EXP_SCALE = 1.4426950408889634 * HEAD_DIM**-0.5
MESH = pl.DeviceIdType.MESH
f32 = jnp.float32
bf16 = jnp.bfloat16


def dot(a, b, dims):
    return lax.dot_general(a, b, (dims, ((), ())), preferred_element_type=f32)


def kernel(
    mask_ref,
    q_ref,
    k_ref,
    v_ref,
    o_ref,
    qg,
    kv,
    half,
    scores,
    state,
    maxima,
    osend,
    orecv,
    ssend,
    srecv,
    info_i,
    info_j,
    info_prev,
    info_thr,
    last,
    own_sem,
    half_sem,
    q_sem,
    ya_sem,
    yb_sem,
    za_send,
    za_recv,
    zb_send,
    zb_recv,
    sib_sem,
    o_sem,
    s_sem,
):
    r = lax.axis_index("row")
    c = lax.axis_index("col")
    core = lax.rem(r, 2)
    zl = lax.rem(r // 2, RING)
    y = r // 8
    x = lax.rem(c, RING)
    z = (c // RING) * RING + zl

    def at_x(d):
        return (r, (c // RING) * RING + lax.rem(x + d, RING))

    def at_y(d):
        return (lax.rem(y + d, RING) * 8 + lax.rem(r, 8), c)

    def at_z(d):
        t = lax.rem(z + d + ZRING, ZRING)
        return (y * 8 + lax.rem(t, RING) * 2 + core, (t // RING) * RING + x)

    sibling = (r + 1 - 2 * core, c)

    def remote(src, dst, send, recv, device):
        return pltpu.make_async_remote_copy(
            src_ref=src, dst_ref=dst, send_sem=send, recv_sem=recv, device_id=device, device_id_type=MESH
        )

    def drain(view, sem):
        pltpu.make_async_copy(view, view, sem).wait()

    barrier = pltpu.get_barrier_semaphore()
    partners = [sibling, at_z(1), at_z(-1)] + [at_x(d) for d in (1, 2, 3)] + [at_y(d) for d in (1, 2, 3)]
    for partner in partners:
        pl.semaphore_signal(barrier, inc=1, device_id=partner, device_id_type=MESH)
    pl.semaphore_wait(barrier, len(partners))

    @pl.when(core == 0)
    def _():
        remote(v_ref, half, half_sem.at[0], half_sem.at[1], sibling).start()

    @pl.when(core == 1)
    def _():
        remote(k_ref, half, half_sem.at[0], half_sem.at[1], sibling).start()

    own = pltpu.make_async_copy(q_ref, qg.at[0], own_sem)
    own.start()
    q_copies = [remote(q_ref, qg.at[RING - d], q_sem.at[0, d], q_sem.at[1, RING - d], at_x(d)) for d in (1, 2, 3)]
    for copy in q_copies:
        copy.start()

    remote(v_ref, half, half_sem.at[0], half_sem.at[1], sibling).wait()

    @pl.when(core == 0)
    def _():
        kv[0, z, y] = jnp.concatenate([k_ref[...], half[...]], axis=0)

    @pl.when(core == 1)
    def _():
        kv[1, z, y] = jnp.concatenate([half[...], v_ref[...]], axis=0).astype(f32).T.astype(bf16)

    lower, upper = pl.ds(0, HALF), pl.ds(HALF, HALF)

    def slab(t):
        return kv.at[core, t, :, lower]

    def piece(t):
        return kv.at[core, t, y, upper]

    def send_slab(t, direction, step):
        remote(
            slab(t), slab(t), za_send.at[direction], za_recv.at[direction, step], at_z(1 - 2 * direction)
        ).start()

    def send_piece(t, direction, step):
        remote(
            piece(t), piece(t), zb_send.at[direction], zb_recv.at[direction, step], at_z(1 - 2 * direction)
        ).start()

    def spread_piece(t):
        for d in (1, 2, 3):
            remote(piece(t), piece(t), yb_sem.at[0], yb_sem.at[1], at_y(d)).start()

    def share_slab(t):
        remote(slab(t), slab(t), sib_sem.at[0], sib_sem.at[1], sibling).start()

    a_copies = [
        remote(kv.at[core, z, y, lower], kv.at[core, z, y, lower], ya_sem.at[0, d], ya_sem.at[1, d], at_y(d))
        for d in (1, 2, 3)
    ]
    for copy in a_copies:
        copy.start()
    for direction in (0, 1):
        send_piece(z, direction, 1)
    spread_piece(z)

    def wait_slab(t, direction, step):
        drain(slab(t), za_recv.at[direction, step])

    def wait_piece(t, direction, step):
        drain(piece(t), zb_recv.at[direction, step])

    for d in (1, 2, 3):
        from_y = lax.rem(y + RING - d, RING)
        drain(kv.at[core, z, from_y, lower], ya_sem.at[1, d])
    for direction in (0, 1):
        send_slab(z, direction, 1)
    share_slab(z)

    for i in (0, 1):
        last[i] = jnp.int32(NSLOT)
    for b in range(RING):
        count = jnp.int32(0)
        found_i = [jnp.int32(0)] * SLOTS
        found_j = [jnp.int32(0)] * SLOTS
        for i in (0, 1):
            for j in range(RING):
                flag = mask_ref[2 * r + i, (b * RING + x) * RING + j]
                for s in range(SLOTS):
                    here = flag * jnp.where(count == s, 1, 0)
                    found_i[s] = found_i[s] + here * i
                    found_j[s] = found_j[s] + here * j
                count = count + flag
        for s in range(SLOTS):
            t = b * SLOTS + s
            active = count > s
            i, j = found_i[s], found_j[s]
            info_i[t] = i
            info_j[t] = j
            info_prev[t] = jnp.where(i == 0, last[0], last[1])
            info_thr[t] = jnp.where(2 * r + i == (b * RING + x) * RING + j, 0, BLOCK)
            last[0] = jnp.where(jnp.logical_and(active, i == 0), t, last[0])
            last[1] = jnp.where(jnp.logical_and(active, i == 1), t, last[1])
    state[NSLOT] = jnp.zeros(state.shape[1:], f32)
    maxima[NSLOT] = jnp.full(maxima.shape[1:], NEG_FILL, f32)

    def ring_step(step, forward_plus, forward_minus, minus):
        plus_t = lax.rem(z - step + ZRING, ZRING)
        minus_t = lax.rem(z + step, ZRING)
        wait_slab(plus_t, 0, step)
        if forward_plus:
            send_slab(plus_t, 0, step + 1)
        if minus:
            wait_slab(minus_t, 1, step)
            if forward_minus:
                send_slab(minus_t, 1, step + 1)
        wait_piece(plus_t, 0, step)
        if forward_plus:
            send_piece(plus_t, 0, step + 1)
        if minus:
            wait_piece(minus_t, 1, step)
            if forward_minus:
                send_piece(minus_t, 1, step + 1)
        spread_piece(plus_t)
        share_slab(plus_t)
        if minus:
            spread_piece(minus_t)
            share_slab(minus_t)

    def ring_body(step, carry):
        ring_step(step, True, True, True)
        return carry

    lax.fori_loop(1, ZRING // 2 - 1, ring_body, 0)
    ring_step(ZRING // 2 - 1, True, False, True)
    ring_step(ZRING // 2, False, False, False)

    drain(kv.at[core, :, pl.ds(0, 3), upper], yb_sem.at[1])
    uppers = remote(
        kv.at[core, :, :, upper], kv.at[core, :, :, upper], sib_sem.at[2], sib_sem.at[3], sibling
    )
    uppers.start()
    drain(kv.at[1 - core, :, :, lower], sib_sem.at[1])
    own.wait()
    for d in (1, 2, 3):
        q_copies[d - 1].wait_recv()
    drain(kv.at[1 - core, :, :, upper], sib_sem.at[3])

    ones = jnp.ones((SUMROWS, BLOCK), bf16)
    offset = lax.broadcasted_iota(jnp.int32, (BLOCK, BLOCK), 0) - lax.broadcasted_iota(
        jnp.int32, (BLOCK, BLOCK), 1
    )

    def score(head, t):
        b4 = (t // SLOTS) * RING
        keys = jnp.concatenate([kv[0, b4 + n, info_j[t]] for n in range(RING)], axis=0)
        return dot(keys, qg[head, info_i[t]], ((1,), (1,)))

    def soften(t, s, masked):
        b4 = (t // SLOTS) * RING
        prev = info_prev[t]
        if masked:
            s = jnp.where(offset <= info_thr[t], s, NEG_FILL)
        old_max = maxima[prev]
        new_max = jnp.maximum(old_max, jnp.max(s, axis=0, keepdims=True))
        factor = jnp.exp2((old_max - new_max) * EXP_SCALE)
        weights = jnp.exp2((s - new_max) * EXP_SCALE).astype(bf16)
        values = jnp.concatenate([kv[1, b4 + n, info_j[t]] for n in range(RING)], axis=1)
        values = jnp.concatenate([values, ones], axis=0)
        maxima[t] = new_max
        state[t] = state[prev] * factor + dot(values, weights, ((1,), (0,)))

    def stretch(head, b, masked):
        for s in range(SLOTS):
            t = b * SLOTS + s
            following = jnp.minimum(t + 1, NSLOT - 1)
            scores[(s + 1) % SLOTS] = score(head, following)
            soften(t, scores[s], masked)

    def head_body(n, carry):
        head = lax.rem(n + 1, RING)
        scores[0] = score(head, 0)

        def stretch_body(b, inner):
            stretch(head, b, False)
            return inner

        lax.fori_loop(0, y, stretch_body, 0)

        @pl.when(x <= zl)
        def _():
            stretch(head, y, True)

        for i in (0, 1):
            final = state[last[i]]
            osend[head, i] = final[:HEAD_DIM].astype(bf16)
            ssend[head, pl.ds(2 * i, 1)] = maxima[last[i]]
            ssend[head, pl.ds(2 * i + 1, 1)] = final[HEAD_DIM : HEAD_DIM + 1]

        @pl.when(n < RING - 1)
        def _():
            slot = RING - head
            remote(osend.at[head], orecv.at[slot - 1], o_sem.at[0, head], o_sem.at[1, slot], at_x(head)).start()
            remote(ssend.at[head], srecv.at[slot - 1], s_sem.at[0, head], s_sem.at[1, slot], at_x(head)).start()

        return carry

    lax.fori_loop(0, RING, head_body, 0)

    for d in (1, 2, 3):
        drain(orecv.at[d - 1], o_sem.at[1, d])
        drain(srecv.at[d - 1], s_sem.at[1, d])
    for i in (0, 1):
        stats = [ssend[0]] + [srecv[n] for n in range(RING - 1)]
        parts = [osend[0, i]] + [orecv[n, i] for n in range(RING - 1)]
        tops = [a[2 * i : 2 * i + 1] for a in stats]
        totals = [a[2 * i + 1 : 2 * i + 2] for a in stats]
        top = jnp.maximum(jnp.maximum(tops[0], tops[1]), jnp.maximum(tops[2], tops[3]))
        shares = [jnp.exp2((a - top) * EXP_SCALE) for a in tops]
        denominator = sum(a * b for a, b in zip(shares, totals))
        out = sum(p.astype(f32) * (a / denominator) for p, a in zip(parts, shares))
        o_ref[pl.ds(i * BLOCK, BLOCK)] = out.T.astype(bf16)

    for d in (1, 2, 3):
        q_copies[d - 1].wait_send()
        a_copies[d - 1].wait_send()
        drain(osend.at[d], o_sem.at[0, d])
        drain(ssend.at[d], s_sem.at[0, d])
    drain(kv.at[core, :, pl.ds(0, 3), upper], yb_sem.at[0])
    drain(kv.at[core, pl.ds(0, 8), :, lower], za_send.at[0])
    drain(kv.at[core, pl.ds(0, 7), :, lower], za_send.at[1])
    drain(kv.at[core, pl.ds(0, 8), y, upper], zb_send.at[0])
    drain(kv.at[core, pl.ds(0, 7), y, upper], zb_send.at[1])
    drain(kv.at[core, :, :, lower], sib_sem.at[0])
    uppers.wait_send()


def body(queries, key_vectors, value_vectors, block_mask):
    rows, width = queries.shape
    vmem = pl.BlockSpec(memory_space=pltpu.VMEM)
    dma = pltpu.SemaphoreType.DMA
    return pl.pallas_call(
        kernel,
        out_shape=jax.ShapeDtypeStruct((rows, width), bf16),
        in_specs=[
            pl.BlockSpec(memory_space=pltpu.SMEM),
            pl.BlockSpec(memory_space=pl.ANY),
            vmem,
            vmem,
        ],
        out_specs=vmem,
        scratch_shapes=[
            pltpu.VMEM((RING, 2, BLOCK, HEAD_DIM), bf16),
            pltpu.VMEM((2, ZRING, RING, PIECE, HEAD_DIM), bf16),
            pltpu.VMEM((HALF, HEAD_DIM), bf16),
            pltpu.VMEM((SLOTS, BLOCK, BLOCK), f32),
            pltpu.VMEM((NSLOT + 1, HEAD_DIM + SUMROWS, BLOCK), f32),
            pltpu.VMEM((NSLOT + 1, 1, BLOCK), f32),
            pltpu.VMEM((RING, 2, HEAD_DIM, BLOCK), bf16),
            pltpu.VMEM((RING - 1, 2, HEAD_DIM, BLOCK), bf16),
            pltpu.VMEM((RING, 8, BLOCK), f32),
            pltpu.VMEM((RING - 1, 8, BLOCK), f32),
            pltpu.SMEM((NSLOT,), jnp.int32),
            pltpu.SMEM((NSLOT,), jnp.int32),
            pltpu.SMEM((NSLOT,), jnp.int32),
            pltpu.SMEM((NSLOT,), jnp.int32),
            pltpu.SMEM((2,), jnp.int32),
            dma,
            dma((2,)),
            dma((2, RING)),
            dma((2, RING)),
            dma((2,)),
            dma((2,)),
            dma((2, ZRING)),
            dma((2,)),
            dma((2, ZRING)),
            dma((4,)),
            dma((2, RING)),
            dma((2, RING)),
        ],
        compiler_params=pltpu.CompilerParams(
            collective_id=0, has_side_effects=True, vmem_limit_bytes=48 * 2**20
        ),
    )(block_mask, queries.reshape(2, BLOCK, width), key_vectors, value_vectors)


def solution(mesh):
    placed = (P("row", "col"), P(("col", "row"), None), P(("col", "row"), None), P())
    return jax.shard_map(body, mesh=mesh, in_specs=placed, out_specs=P("row", "col"), check_vma=False)
```

time: 615 us -> 78.6 us (0.13)
  the two profiles are of different devices: /device:TPU:24 before, /device:TPU:31 now
where the time goes in v1:
time: 78.6 us; the launch traced here: 78.2 us
  Pallas kernels  74.4 us (95%)
  local copies, waits for them, and re-layouts  3.85 us (5%)
    pallas_call x1, Pallas kernels, body(): pl.pallas_call(kernel, out_shape=jax.ShapeDtypeStruct((rows, width), bf16...  74.4 us
    unnamed x9, local copies, waits for them, and re-layouts  3.85 us

profile of v1, /device:TPU:31, one launch (start us, length us, event | category | flops | bytes accessed | tf_op | source)
XLA Modules:
  0.0 78.2 jit_solution(18092855128694124444)
XLA Ops:
  0.0 0.0 copy-start
  0.0 0.9 %copy-done = bf16[1024,128]{1,0:T(8,128)(2,1)S(1)} copy-done((bf16[1024,128]{1,0:T(8,128)(2,1)S(1)}, bf16[1024,128]{1,0:T(8,128)(2,1)}, u32[]{:S(2)}) %copy-start) | copy-done | bytes 262168
  1.0 0.0 copy-start.1
  1.0 0.8 copy-done.1
  1.7 0.0 copy-start.2
  1.7 0.7 copy-done.2
  2.4 0.0 copy-start.3
  2.4 0.7 copy-done.3
  3.1 74.4 %shard_map.46 = bf16[1024,128]{1,0:T(8,128)(2,1)S(1)} custom-call(s32[64,64]{1,0:T(8,128)S(1)} %copy-done.1, bf16[2,512,128]{2,1,0:T(8,128)(2,1)S(1)} %bitcast.1, bf16[64,128]{1,0:T(8,128)(2,1)S(1)} %copy-done.2, bf16[64,128]{1,0:T(8,128)(2,1)S(1)} %copy-done.3), custom_call_target="tpu_custom_call" | custom-call | tf_op jit(solution)/shard_map/pallas_call | solution.py:330
  77.5 0.7 copy.6
Async XLA Ops:
  0.0 0.9 %copy-start = (bf16[1024,128]{1,0:T(8,128)(2,1)S(1)}, bf16[1024,128]{1,0:T(8,128)(2,1)}, u32[]{:S(2)}) copy-start(bf16[1024,128]{1,0:T(8,128)(2,1)} %param.4) | copy-start | bytes 786436
  1.0 0.8 copy-start.1
  1.7 0.7 copy-start.2
  2.4 0.7 copy-start.3

commit v2 on v1

v2 whole, which is shorter than its diff:
```python
import functools

import jax
import jax.numpy as jnp
from jax import lax
from jax.experimental import pallas as pl
from jax.experimental.pallas import tpu as pltpu
from jax.sharding import PartitionSpec as P

HEAD_DIM = 128
BLOCK = 512
SLOTS = 3
RING = 4
ZRING = 16
NSLOT = SLOTS * RING
PIECE = 128
HALF = 64
SUMROWS = 16
HERE = 8
LAST = 7
ROUNDS = 4
MESSAGES = 6
NEG_FILL = -1e30
NO_CAP = 3e38
EXP_SCALE = 1.4426950408889634 * HEAD_DIM**-0.5
MESH = pl.DeviceIdType.MESH
f32 = jnp.float32
bf16 = jnp.bfloat16


def dot(a, b, dims):
    return lax.dot_general(a, b, (dims, ((), ())), preferred_element_type=f32)


def kernel(
    mask_hbm,
    q_ref,
    k_ref,
    v_ref,
    o_ref,
    mask_ref,
    qg,
    kv,
    raw,
    scores,
    cap,
    near0,
    near1,
    state,
    maxima,
    osend,
    orecv,
    oin,
    ssend,
    srecv,
    sin,
    info_i,
    info_j,
    info_prev,
    info_diag,
    last,
    own_sem,
    near_sem,
    raw_sem,
    far_sem,
    q_sem,
    yb_send,
    yb_recv,
    z_send,
    z_recv,
    sib_send,
    sib_recv,
    o_sem,
    s_sem,
):
    r = lax.axis_index("row")
    c = lax.axis_index("col")
    core = lax.rem(r, 2)
    zl = lax.rem(r // 2, RING)
    y = r // 8
    x = lax.rem(c, RING)
    z = (c // RING) * RING + zl
    parity, plane = lax.rem(y, 2), y // 2

    def at_x(d):
        return (r, (c // RING) * RING + lax.rem(x + d, RING))

    def at_y(d):
        return (lax.rem(y + d, RING) * 8 + lax.rem(r, 8), c)

    def at_z(d):
        t = lax.rem(z + d + ZRING, ZRING)
        return (y * 8 + lax.rem(t, RING) * 2 + core, (t // RING) * RING + x)

    sibling = (r + 1 - 2 * core, c)
    far = at_y(2)
    far_sibling = (far[0] + 1 - 2 * core, c)

    def remote(src, dst, send, recv, device):
        return pltpu.make_async_remote_copy(
            src_ref=src, dst_ref=dst, send_sem=send, recv_sem=recv, device_id=device, device_id_type=MESH
        )

    def drain(view, sem):
        pltpu.make_async_copy(view, view, sem).wait()

    own_k = pltpu.make_async_copy(k_ref, kv.at[HERE, parity, core, 0, plane], own_sem.at[0])
    own_v = pltpu.make_async_copy(v_ref, raw.at[0, core], own_sem.at[1])
    own_q = pltpu.make_async_copy(q_ref, qg.at[0], own_sem.at[2])
    own_mask = pltpu.make_async_copy(mask_hbm, mask_ref, own_sem.at[3])
    for copy in (own_k, own_v, own_q, own_mask):
        copy.start()

    barrier = pltpu.get_barrier_semaphore()
    partners = [sibling, far_sibling] + [at_z(d) for d in (1, -1, 2, -2)]
    partners += [at_x(d) for d in (1, 2, 3)] + [at_y(d) for d in (1, 2, 3)]
    for partner in partners:
        pl.semaphore_signal(barrier, inc=1, device_id=partner, device_id_type=MESH)
    pl.semaphore_wait(barrier, len(partners))

    first_copies = [
        remote(k_ref, kv.at[HERE, parity, core, 0, plane], far_sem.at[0], far_sem.at[1], far),
        remote(v_ref, raw.at[0, core], raw_sem.at[0, 0], raw_sem.at[1, 0], sibling),
        remote(v_ref, raw.at[1, core], raw_sem.at[0, 1], raw_sem.at[1, 1], far),
        remote(v_ref, raw.at[1, core], raw_sem.at[0, 2], raw_sem.at[1, 2], far_sibling),
    ]
    for copy in first_copies:
        copy.start()
    q_copies = [remote(q_ref, qg.at[RING - d], q_sem.at[0, d], q_sem.at[1, RING - d], at_x(d)) for d in (1, 2, 3)]
    for copy in q_copies:
        copy.start()

    def slab(stream, o):
        return kv.at[HERE + o, parity, core, stream % 2, plane if stream < 2 else 1 - plane]

    def send_z(stream, o, hop):
        remote(
            slab(stream, o), slab(stream, o - hop), z_send.at[stream], z_recv.at[stream, HERE + o - hop], at_z(hop)
        ).start()

    def wait_z(stream, o):
        drain(slab(stream, o), z_recv.at[stream, HERE + o])

    def pieces(first, count, from_y):
        return kv.at[pl.ds(HERE + first, count), lax.rem(from_y, 2), core, :, from_y // 2]

    def spread(n, way, first, count):
        for d in (1, 3):
            view = pieces(first, count, y)
            remote(view, view, yb_send, yb_recv.at[n, way, d // 2], at_y(d)).start()

    def gathered(n, way, first, count):
        for d in (1, 3):
            drain(pieces(first, count, lax.rem(y + RING - d, RING)), yb_recv.at[n, way, d // 2])

    def shared(first, count, of_core):
        return kv.at[pl.ds(HERE + first, count), :, of_core]

    def share(n, way, first, count):
        view = shared(first, count, core)
        remote(view, view, sib_send, sib_recv.at[n, way], sibling).start()

    def arrivals(n):
        if n == 0:
            return [(0, 0, 1)]
        return [(0, -2 * n, 2), (1, 2 * n - 1, 2 if n < ROUNDS else 1)]

    own_k.wait()
    for hop in (2, -2, 1, -1):
        send_z(0, 0, hop)
    own_v.wait()
    drain(raw.at[0, 1 - core], raw_sem.at[1, 0])
    own_turned = raw[0].reshape(PIECE, HEAD_DIM).astype(f32).T.astype(bf16)
    for i in (0, 1):

        @pl.when(core == i)
        def _():
            kv[HERE, parity, i, 1, plane] = own_turned[i * HALF : (i + 1) * HALF]

    for hop in (2, -2, 1, -1):
        send_z(1, 0, hop)
    drain(kv.at[HERE, parity, core, 0, 1 - plane], far_sem.at[1])
    for hop in (2, -2, 1, -1):
        send_z(2, 0, hop)
    drain(raw.at[1, core], raw_sem.at[1, 1])
    drain(raw.at[1, 1 - core], raw_sem.at[1, 2])
    far_turned = raw[1].reshape(PIECE, HEAD_DIM).astype(f32).T.astype(bf16)
    for i in (0, 1):

        @pl.when(core == i)
        def _():
            kv[HERE, parity, i, 1, 1 - plane] = far_turned[i * HALF : (i + 1) * HALF]

    for hop in (2, -2, 1, -1):
        send_z(3, 0, hop)
    spread(0, 0, 0, 1)
    own_mask.wait()

    zh = c // RING

    def valid(b):
        return b * RING + x <= r // 2

    side = jnp.where(zl < 2, 3, 1)
    third, fourth = lax.rem(zh + RING - side, RING), lax.rem(zh + 2, RING)
    order = [
        zh,
        lax.rem(zh + side, RING),
        jnp.where(valid(third), third, fourth),
        jnp.where(valid(third), fourth, third),
    ]
    n_late = valid(third).astype(jnp.int32) + valid(fourth).astype(jnp.int32)

    for i in (0, 1):
        last[i] = jnp.int32(NSLOT)
    for place, b in enumerate(order):
        count = jnp.int32(0)
        found_i = [jnp.int32(0)] * SLOTS
        found_j = [jnp.int32(0)] * SLOTS
        for i in (0, 1):
            for j in range(RING):
                flag = mask_ref[2 * r + i, (b * RING + x) * RING + j]
                for s in range(SLOTS):
                    here = flag * jnp.where(count == s, 1, 0)
                    found_i[s] = found_i[s] + here * i
                    found_j[s] = found_j[s] + here * j
                count = count + flag
        for s in range(SLOTS):
            t = place * SLOTS + s
            active = count > s
            i, j = found_i[s], found_j[s]
            info_i[t] = i
            info_j[t] = j
            info_prev[t] = jnp.where(i == 0, last[0], last[1])
            info_diag[t] = jnp.where(2 * r + i == (b * RING + x) * RING + j, 1, 0)
            last[0] = jnp.where(jnp.logical_and(active, i == 0), t, last[0])
            last[1] = jnp.where(jnp.logical_and(active, i == 1), t, last[1])
    key_at = lax.broadcasted_iota(jnp.int32, (BLOCK, BLOCK), 0)
    query_at = lax.broadcasted_iota(jnp.int32, (BLOCK, BLOCK), 1)
    cap[0] = jnp.full((BLOCK, BLOCK), NO_CAP, f32)
    cap[1] = jnp.where(key_at <= query_at, NO_CAP, NEG_FILL)
    for head in range(RING):
        state[head, NSLOT] = jnp.zeros(state.shape[2:], f32)
        maxima[head, NSLOT] = jnp.full(maxima.shape[2:], NEG_FILL, f32)

    ones = jnp.ones((SUMROWS, BLOCK), bf16)

    def late_tile(kind, t, n):
        b = jnp.where(t < 3 * SLOTS, order[2], order[3])
        j = info_j[t]
        return kv[lax.rem(b * RING + n - z + HERE + ZRING, ZRING), lax.rem(j, 2), :, kind, j // 2]

    def near_tile(near):
        def tile(kind, t, n):
            j = info_j[t]
            return near[n, lax.rem(j, 2), :, kind, j // 2]

        return tile

    def score(tile, head, t):
        keys = jnp.concatenate([tile(0, t, n).reshape(PIECE, HEAD_DIM) for n in range(RING)], axis=0)
        return dot(keys, qg[head, info_i[t]], ((1,), (1,)))

    def soften(tile, head, t, s):
        prev = info_prev[t]
        s = jnp.minimum(s, cap[info_diag[t]])
        old_max = maxima[head, prev]
        new_max = jnp.maximum(old_max, jnp.max(s, axis=0, keepdims=True))
        factor = jnp.exp2((old_max - new_max) * EXP_SCALE)
        weights = jnp.exp2((s - new_max) * EXP_SCALE).astype(bf16)
        values = jnp.concatenate([tile(1, t, n).reshape(PIECE, HEAD_DIM) for n in range(RING)], axis=1)
        values = jnp.concatenate([values, ones], axis=0)
        maxima[head, t] = new_max
        state[head, t] = state[head, prev] * factor + dot(values, weights, ((1,), (0,)))

    def stretch(tile, head, t, next_head, next_t):
        for s in range(SLOTS):
            if s < SLOTS - 1:
                scores[s + 1] = score(tile, head, t + s + 1)
            else:
                scores[0] = score(tile, next_head, next_t)
            soften(tile, head, t + s, scores[s])

    def early(near, place, first, count):
        tile, t = near_tile(near), place * SLOTS

        @pl.when(valid(order[place]))
        def _():
            scores[0] = score(tile, first, t)

            def head_body(head, carry):
                stretch(tile, head, t, lax.rem(head + 1, RING), t)
                return carry

            lax.fori_loop(first, first + count, head_body, 0)

    def bring(near, place):
        first = lax.rem(order[place] * RING - z + HERE + ZRING, ZRING)
        return pltpu.make_async_copy(kv.at[pl.ds(first, RING)], near, near_sem.at[place])

    def wait_shared(n):
        for way, first, count in arrivals(n):
            drain(shared(first, count, 1 - core), sib_recv.at[n, way])

    for n in range(1, ROUNDS + 1):
        for hops in ((2, -2), (1, -1)):
            for stream in range(4):
                for hop in hops:
                    o = -2 * n if hop > 0 else 2 * n
                    if n < ROUNDS and abs(hop) == 2:
                        wait_z(stream, o)
                    if n < ROUNDS and o - hop <= LAST:
                        send_z(stream, o, hop)
        for way, first, count in arrivals(n):
            for o in range(first, first + count):
                if n == ROUNDS or abs(o) % 2:
                    for stream in range(4):
                        wait_z(stream, o)
            spread(n, way, first, count)
        for way, first, count in arrivals(n - 1):
            gathered(n - 1, way, first, count)
            share(n - 1, way, first, count)
        if n == ROUNDS - 1:
            own_q.wait()
            for d in (1, 2, 3):
                q_copies[d - 1].wait_recv()
            for m in range(n):
                wait_shared(m)
            copy = bring(near0, 0)
            copy.start()
            copy.wait()
            early(near0, 0, 0, 2)
    early(near0, 0, 2, 2)
    for way, first, count in arrivals(ROUNDS):
        gathered(ROUNDS, way, first, count)
        share(ROUNDS, way, first, count)
    wait_shared(ROUNDS - 1)
    copy = bring(near1, 1)
    copy.start()
    copy.wait()
    early(near1, 1, 0, 4)
    wait_shared(ROUNDS)

    def message(m):
        head, i, to, into = (
            (2, 0, 1, oin.at[0]),
            (2, 1, 3, oin.at[1]),
            (1, 1, 1, orecv.at[0, 1]),
            (3, 0, 3, orecv.at[1, 0]),
            (1, 0, 1, orecv.at[0, 0]),
            (3, 1, 3, orecv.at[1, 1]),
        )[m]
        stats = (sin.at[0], sin.at[1], srecv.at[0, 1], srecv.at[1, 0], srecv.at[0, 0], srecv.at[1, 1])[m]
        return (
            remote(osend.at[head, i], into, o_sem.at[0, m], o_sem.at[1, m], at_x(to)),
            remote(ssend.at[head, i], stats, s_sem.at[0, m], s_sem.at[1, m], at_x(to)),
        )

    def send(*messages):
        for m in messages:
            for copy in message(m):
                copy.start()

    def arrived(*messages):
        for m in messages:
            for copy in message(m):
                copy.wait_recv()

    def merged(parts):
        tops = [stats[0:1] for _, stats in parts]
        top = functools.reduce(jnp.maximum, tops)
        shares = [jnp.exp2((a - top) * EXP_SCALE) for a in tops]
        total = sum(stats[1:2] * a for (_, stats), a in zip(parts, shares))
        return [p.astype(f32) for p, _ in parts], shares, top, total

    def head_of(n):
        return jnp.where(n == 0, 2, jnp.where(n == 1, 1, jnp.where(n == 2, 3, 0)))

    late = 2 * SLOTS
    scores[0] = score(late_tile, head_of(0), late)

    def head_body(n, carry):
        head = head_of(n)

        def stretch_body(place, inner):
            done = place == n_late - 1
            stretch(
                late_tile,
                head,
                late + place * SLOTS,
                jnp.where(done, head_of(n + 1), head),
                jnp.where(done, late, jnp.minimum(late + (place + 1) * SLOTS, NSLOT - 1)),
            )
            return inner

        lax.fori_loop(0, n_late, stretch_body, 0)
        for i in (0, 1):
            final = state[head, last[i]]
            osend[head, i] = final[:HEAD_DIM].astype(bf16)
            ssend[head, i, 0:1] = maxima[head, last[i]]
            ssend[head, i, 1:2] = final[HEAD_DIM : HEAD_DIM + 1]

        @pl.when(n == 0)
        def _():
            send(0, 1)

        @pl.when(n == 1)
        def _():
            send(2)

        @pl.when(n == 2)
        def _():
            send(3)

        return carry

    lax.fori_loop(0, RING, head_body, 0)
    arrived(0, 1)
    for head, i in ((1, 0), (3, 1)):
        parts = [(osend[head, i], ssend[head, i]), (oin[i], sin[i])]
        values, shares, top, total = merged(parts)
        osend[head, i] = sum(p * a for p, a in zip(values, shares)).astype(bf16)
        ssend[head, i, 0:1] = top
        ssend[head, i, 1:2] = total
    send(4, 5)
    arrived(2, 3, 4, 5)
    for i in (0, 1):
        parts = [(osend[0, i], ssend[0, i]), (orecv[0, i], srecv[0, i]), (orecv[1, i], srecv[1, i])]
        values, shares, top, total = merged(parts)
        o_ref[i] = sum(p * (a / total) for p, a in zip(values, shares)).astype(bf16)

    for d in (1, 2, 3):
        q_copies[d - 1].wait_send()
    for m in range(MESSAGES):
        for copy in message(m):
            copy.wait_send()
    for copy in first_copies:
        copy.wait_send()
    drain(kv.at[:, :, core, :, 0], yb_send)
    for stream in range(4):
        drain(kv.at[pl.ds(0, ZRING - 1), parity, core, 0, 0], z_send.at[stream])
    drain(kv.at[:, :, core], sib_send)


def body(queries, key_vectors, value_vectors, block_mask):
    rows, width = queries.shape
    vmem = pl.BlockSpec(memory_space=pltpu.VMEM)
    dma = pltpu.SemaphoreType.DMA
    turned = pl.pallas_call(
        kernel,
        out_shape=jax.ShapeDtypeStruct((2, width, BLOCK), bf16),
        in_specs=[pl.BlockSpec(memory_space=pltpu.HBM)] * 4,
        out_specs=vmem,
        scratch_shapes=[
            pltpu.SMEM(block_mask.shape, jnp.int32),
            pltpu.VMEM((RING, 2, BLOCK, HEAD_DIM), bf16),
            pltpu.VMEM((ZRING, 2, 2, 2, 2, HALF, HEAD_DIM), bf16),
            pltpu.VMEM((2, 2, HALF, HEAD_DIM), bf16),
            pltpu.VMEM((SLOTS, BLOCK, BLOCK), f32),
            pltpu.VMEM((2, BLOCK, BLOCK), f32),
            pltpu.VMEM((RING, 2, 2, 2, 2, HALF, HEAD_DIM), bf16),
            pltpu.VMEM((RING, 2, 2, 2, 2, HALF, HEAD_DIM), bf16),
            pltpu.VMEM((RING, NSLOT + 1, HEAD_DIM + SUMROWS, BLOCK), f32),
            pltpu.VMEM((RING, NSLOT + 1, 1, BLOCK), f32),
            pltpu.VMEM((RING, 2, HEAD_DIM, BLOCK), bf16),
            pltpu.VMEM((2, 2, HEAD_DIM, BLOCK), bf16),
            pltpu.VMEM((2, HEAD_DIM, BLOCK), bf16),
            pltpu.VMEM((RING, 2, 8, BLOCK), f32),
            pltpu.VMEM((2, 2, 8, BLOCK), f32),
            pltpu.VMEM((2, 8, BLOCK), f32),
            pltpu.SMEM((NSLOT,), jnp.int32),
            pltpu.SMEM((NSLOT,), jnp.int32),
            pltpu.SMEM((NSLOT,), jnp.int32),
            pltpu.SMEM((NSLOT,), jnp.int32),
            pltpu.SMEM((2,), jnp.int32),
            dma((4,)),
            dma((2,)),
            dma((2, 3)),
            dma((2,)),
            dma((2, RING)),
            dma,
            dma((ROUNDS + 1, 2, 2)),
            dma((4,)),
            dma((4, ZRING)),
            dma,
            dma((ROUNDS + 1, 2)),
            dma((2, MESSAGES)),
            dma((2, MESSAGES)),
        ],
        compiler_params=pltpu.CompilerParams(
            collective_id=0, has_side_effects=True, vmem_limit_bytes=58 * 2**20
        ),
    )(block_mask, queries.reshape(2, BLOCK, width), key_vectors, value_vectors)
    return turned.transpose(0, 2, 1).reshape(rows, width)


def solution(mesh):
    placed = (P("row", "col"), P(("col", "row"), None), P(("col", "row"), None), P())
    return jax.shard_map(body, mesh=mesh, in_specs=placed, out_specs=P("row", "col"), check_vma=False)
```

time: 78.6 us -> 62.3 us (0.79)
  the two profiles are of different devices: /device:TPU:31 before, /device:TPU:30 now
where the time goes in v2:
time: 62.3 us; the launch traced here: 62.2 us
  Pallas kernels  60.4 us (97%)
  local copies, waits for them, and re-layouts  1.79 us (3%)
    pallas_call x1, Pallas kernels, body(): pl.pallas_call(kernel, out_shape=jax.ShapeDtypeStruct((2, width, BLOCK),...  60.4 us
    transpose x1, local copies, waits for them, and re-layouts, body(): return turned.transpose(0, 2, 1).reshape(rows, width)  1.79 us

profile of v2, /device:TPU:30, one launch (start us, length us, event | category | flops | bytes accessed | tf_op | source)
XLA Modules:
  0.0 62.2 jit_solution(9968107966616582392)
XLA Ops:
  0.0 60.4 %shard_map.46 = bf16[2,128,512]{2,1,0:T(8,128)(2,1)} custom-call(s32[64,64]{1,0:T(8,128)} %mask_hbm.1, bf16[2,512,128]{2,1,0:T(8,128)(2,1)} %bitcast.4, bf16[64,128]{1,0:T(8,128)(2,1)} %k_ref.1, bf16[64,128]{1,0:T(8,128)(2,1)} %v_ref.1), custom_call_target="tpu_custom_call" | custom-call | tf_op jit(solution)/shard_map/pallas_call | solution.py:449
  60.4 1.8 %copy.5 = bf16[2,512,128]{2,1,0:T(8,128)(2,1)} copy(bf16[2,512,128]{1,2,0:T(8,128)(2,1)} %bitcast.3) | data formatting | bytes 524288 | tf_op jit(solution)/shard_map/transpose | solution.py:494

commit v3 on v2

--- a/solution.py
+++ b/solution.py
@@ -20,6 +20,7 @@
 LAST = 7
 ROUNDS = 4
 MESSAGES = 6
+EARLY = 2
 NEG_FILL = -1e30
 NO_CAP = 3e38
 EXP_SCALE = 1.4426950408889634 * HEAD_DIM**-0.5
@@ -133,9 +134,9 @@
     def slab(stream, o):
         return kv.at[HERE + o, parity, core, stream % 2, plane if stream < 2 else 1 - plane]
 
-    def send_z(stream, o, hop):
+    def send_z(stream, o, hop, source=None):
         remote(
-            slab(stream, o), slab(stream, o - hop), z_send.at[stream], z_recv.at[stream, HERE + o - hop], at_z(hop)
+            slab(stream, o) if source is None else source, slab(stream, o - hop), z_send.at[stream], z_recv.at[stream, HERE + o - hop], at_z(hop)
         ).start()
 
     def wait_z(stream, o):
@@ -165,9 +166,9 @@
             return [(0, 0, 1)]
         return [(0, -2 * n, 2), (1, 2 * n - 1, 2 if n < ROUNDS else 1)]
 
+    for hop in (2, -2, 1, -1):
+        send_z(0, 0, hop, k_ref)
     own_k.wait()
-    for hop in (2, -2, 1, -1):
-        send_z(0, 0, hop)
     own_v.wait()
     drain(raw.at[0, 1 - core], raw_sem.at[1, 0])
     own_turned = raw[0].reshape(PIECE, HEAD_DIM).astype(f32).T.astype(bf16)
@@ -194,12 +195,14 @@
     for hop in (2, -2, 1, -1):
         send_z(3, 0, hop)
     spread(0, 0, 0, 1)
-    own_mask.wait()
 
     zh = c // RING
 
     def valid(b):
         return b * RING + x <= r // 2
+
+    def on_diagonal(b):
+        return b * RING + x == r // 2
 
     side = jnp.where(zl < 2, 3, 1)
     third, fourth = lax.rem(zh + RING - side, RING), lax.rem(zh + 2, RING)
@@ -211,42 +214,46 @@
     ]
     n_late = valid(third).astype(jnp.int32) + valid(fourth).astype(jnp.int32)
 
-    for i in (0, 1):
-        last[i] = jnp.int32(NSLOT)
-    for place, b in enumerate(order):
-        count = jnp.int32(0)
-        found_i = [jnp.int32(0)] * SLOTS
-        found_j = [jnp.int32(0)] * SLOTS
+    def prepare():
         for i in (0, 1):
-            for j in range(RING):
-                flag = mask_ref[2 * r + i, (b * RING + x) * RING + j]
-                for s in range(SLOTS):
-                    here = flag * jnp.where(count == s, 1, 0)
-                    found_i[s] = found_i[s] + here * i
-                    found_j[s] = found_j[s] + here * j
-                count = count + flag
-        for s in range(SLOTS):
-            t = place * SLOTS + s
-            active = count > s
-            i, j = found_i[s], found_j[s]
-            info_i[t] = i
-            info_j[t] = j
-            info_prev[t] = jnp.where(i == 0, last[0], last[1])
-            info_diag[t] = jnp.where(2 * r + i == (b * RING + x) * RING + j, 1, 0)
-            last[0] = jnp.where(jnp.logical_and(active, i == 0), t, last[0])
-            last[1] = jnp.where(jnp.logical_and(active, i == 1), t, last[1])
-    key_at = lax.broadcasted_iota(jnp.int32, (BLOCK, BLOCK), 0)
-    query_at = lax.broadcasted_iota(jnp.int32, (BLOCK, BLOCK), 1)
-    cap[0] = jnp.full((BLOCK, BLOCK), NO_CAP, f32)
-    cap[1] = jnp.where(key_at <= query_at, NO_CAP, NEG_FILL)
-    for head in range(RING):
-        state[head, NSLOT] = jnp.zeros(state.shape[2:], f32)
-        maxima[head, NSLOT] = jnp.full(maxima.shape[2:], NEG_FILL, f32)
+            last[i] = jnp.int32(NSLOT)
+        for place, b in enumerate(order):
+            count = jnp.int32(0)
+            found_i = [jnp.int32(0)] * SLOTS
+            found_j = [jnp.int32(0)] * SLOTS
+            for i in (0, 1):
+                for j in range(RING):
+                    flag = mask_ref[2 * r + i, (b * RING + x) * RING + j]
+                    for s in range(SLOTS):
+                        here = flag * jnp.where(count == s, 1, 0)
+                        found_i[s] = found_i[s] + here * i
+                        found_j[s] = found_j[s] + here * j
+                    count = count + flag
+            for s in range(SLOTS):
+                t = place * SLOTS + s
+                active = count > s
+                i, j = found_i[s], found_j[s]
+                info_i[t] = i
+                info_j[t] = j
+                info_prev[t] = jnp.where(i == 0, last[0], last[1])
+                info_diag[t] = jnp.where(2 * r + i == (b * RING + x) * RING + j, 1, 0)
+                last[0] = jnp.where(jnp.logical_and(active, i == 0), t, last[0])
+                last[1] = jnp.where(jnp.logical_and(active, i == 1), t, last[1])
+        key_at = lax.broadcasted_iota(jnp.int32, (BLOCK, BLOCK), 0)
+        query_at = lax.broadcasted_iota(jnp.int32, (BLOCK, BLOCK), 1)
+        cap[0] = jnp.full((BLOCK, BLOCK), NO_CAP, f32)
+        cap[1] = jnp.where(key_at <= query_at, NO_CAP, NEG_FILL)
+        for head in range(RING):
+            state[head, NSLOT] = jnp.zeros(state.shape[2:], f32)
+            maxima[head, NSLOT] = jnp.full(maxima.shape[2:], NEG_FILL, f32)
 
     ones = jnp.ones((SUMROWS, BLOCK), bf16)
 
+    def at_place(place):
+        return jnp.where(place == 1, order[1], jnp.where(place == 2, order[2], order[3]))
+
     def late_tile(kind, t, n):
-        b = jnp.where(t < 3 * SLOTS, order[2], order[3])
+        b = at_place(t // SLOTS)
         j = info_j[t]
         return kv[lax.rem(b * RING + n - z + HERE + ZRING, ZRING), lax.rem(j, 2), :, kind, j // 2]
 
@@ -261,9 +268,10 @@
         keys = jnp.concatenate([tile(0, t, n).reshape(PIECE, HEAD_DIM) for n in range(RING)], axis=0)
         return dot(keys, qg[head, info_i[t]], ((1,), (1,)))
 
-    def soften(tile, head, t, s):
+    def soften(tile, head, t, s, masked):
         prev = info_prev[t]
-        s = jnp.minimum(s, cap[info_diag[t]])
+        if masked:
+            s = jnp.minimum(s, cap[info_diag[t]])
         old_max = maxima[head, prev]
         new_max = jnp.maximum(old_max, jnp.max(s, axis=0, keepdims=True))
         factor = jnp.exp2((old_max - new_max) * EXP_SCALE)
@@ -273,26 +281,32 @@
         maxima[head, t] = new_max
         state[head, t] = state[head, prev] * factor + dot(values, weights, ((1,), (0,)))
 
-    def stretch(tile, head, t, next_head, next_t):
+    def stretch(tile, head, t, next_head, next_t, masked):
         for s in range(SLOTS):
             if s < SLOTS - 1:
                 scores[s + 1] = score(tile, head, t + s + 1)
             else:
                 scores[0] = score(tile, next_head, next_t)
-            soften(tile, head, t + s, scores[s])
-
-    def early(near, place, first, count):
+            soften(tile, head, t + s, scores[s], masked)
+
+    def head_of(n):
+        return jnp.where(n == 0, 2, jnp.where(n == 1, 1, jnp.where(n == 2, 3, 0)))
+
+    def early(near, place, count):
         tile, t = near_tile(near), place * SLOTS
 
-        @pl.when(valid(order[place]))
-        def _():
-            scores[0] = score(tile, first, t)
-
-            def head_body(head, carry):
-                stretch(tile, head, t, lax.rem(head + 1, RING), t)
+        def heads(masked):
+            scores[0] = score(tile, head_of(0), t)
+
+            def head_body(n, carry):
+                stretch(tile, head_of(n), t, head_of(n + 1), t, masked)
                 return carry
 
-            lax.fori_loop(first, first + count, head_body, 0)
+            lax.fori_loop(0, count, head_body, 0)
+
+        on = on_diagonal(order[place])
+        pl.when(jnp.logical_and(valid(order[place]), jnp.logical_not(on)))(lambda: heads(False))
+        pl.when(jnp.logical_and(valid(order[place]), on))(lambda: heads(True))
 
     def bring(near, place):
         first = lax.rem(order[place] * RING - z + HERE + ZRING, ZRING)
@@ -320,6 +334,9 @@
         for way, first, count in arrivals(n - 1):
             gathered(n - 1, way, first, count)
             share(n - 1, way, first, count)
+        if n == 1:
+            own_mask.wait()
+            prepare()
         if n == ROUNDS - 1:
             own_q.wait()
             for d in (1, 2, 3):
@@ -329,8 +346,7 @@
             copy = bring(near0, 0)
             copy.start()
             copy.wait()
-            early(near0, 0, 0, 2)
-    early(near0, 0, 2, 2)
+    early(near0, 0, RING)
     for way, first, count in arrivals(ROUNDS):
         gathered(ROUNDS, way, first, count)
         share(ROUNDS, way, first, count)
@@ -338,7 +354,7 @@
     copy = bring(near1, 1)
     copy.start()
     copy.wait()
-    early(near1, 1, 0, 4)
+    early(near1, 1, EARLY)
     wait_shared(ROUNDS)
 
     def message(m):
@@ -373,27 +389,33 @@
         total = sum(stats[1:2] * a for (_, stats), a in zip(parts, shares))
         return [p.astype(f32) for p, _ in parts], shares, top, total
 
-    def head_of(n):
-        return jnp.where(n == 0, 2, jnp.where(n == 1, 1, jnp.where(n == 2, 3, 0)))
-
-    late = 2 * SLOTS
-    scores[0] = score(late_tile, head_of(0), late)
+    def first_of(n):
+        return jnp.where(jnp.logical_and(n >= EARLY, valid(order[1])), 1, 2)
+
+    scores[0] = score(late_tile, head_of(0), first_of(0) * SLOTS)
 
     def head_body(n, carry):
         head = head_of(n)
 
+        @pl.when(n_late == 0)
+        def _():
+            scores[0] = score(late_tile, head, first_of(n) * SLOTS)
+
         def stretch_body(place, inner):
-            done = place == n_late - 1
-            stretch(
+            done = place == n_late + 1
+            slots = (
                 late_tile,
                 head,
-                late + place * SLOTS,
+                place * SLOTS,
                 jnp.where(done, head_of(n + 1), head),
-                jnp.where(done, late, jnp.minimum(late + (place + 1) * SLOTS, NSLOT - 1)),
+                jnp.where(done, first_of(n + 1), jnp.minimum(place + 1, RING - 1)) * SLOTS,
             )
+            on = on_diagonal(at_place(place))
+            pl.when(jnp.logical_not(on))(lambda: stretch(*slots, False))
+            pl.when(on)(lambda: stretch(*slots, True))
             return inner
 
-        lax.fori_loop(0, n_late, stretch_body, 0)
+        lax.fori_loop(first_of(n), n_late + 2, stretch_body, 0)
         for i in (0, 1):
             final = state[head, last[i]]
             osend[head, i] = final[:HEAD_DIM].astype(bf16)
@@ -411,18 +433,18 @@
         @pl.when(n == 2)
         def _():
             send(3)
+            arrived(0, 1)
+            for m, other, i in ((4, 1, 0), (5, 3, 1)):
+                parts = [(osend[other, i], ssend[other, i]), (oin[i], sin[i])]
+                values, shares, top, total = merged(parts)
+                osend[other, i] = sum(p * a for p, a in zip(values, shares)).astype(bf16)
+                ssend[other, i, 0:1] = top
+                ssend[other, i, 1:2] = total
+                send(m)
 
         return carry
 
     lax.fori_loop(0, RING, head_body, 0)
-    arrived(0, 1)
-    for head, i in ((1, 0), (3, 1)):
-        parts = [(osend[head, i], ssend[head, i]), (oin[i], sin[i])]
-        values, shares, top, total = merged(parts)
-        osend[head, i] = sum(p * a for p, a in zip(values, shares)).astype(bf16)
-        ssend[head, i, 0:1] = top
-        ssend[head, i, 1:2] = total
-    send(4, 5)
     arrived(2, 3, 4, 5)
     for i in (0, 1):
         parts = [(osend[0, i], ssend[0, i]), (orecv[0, i], srecv[0, i]), (orecv[1, i], srecv[1, i])]

time: 62.3 us -> 60 us (0.963)
  Pallas kernels: 60.4 us -> 58.1 us
    pallas_call x1, Pallas kernels: 60.4 us -> 58.1 us  [body(): pl.pallas_call(kernel, out_shape=jax.ShapeDtypeStruct((2, width, BLOCK),...]
where the time goes in v3:
time: 60 us; the launch traced here: 59.9 us
  Pallas kernels  58.1 us (97%)
  local copies, waits for them, and re-layouts  1.79 us (3%)
    pallas_call x1, Pallas kernels, body(): pl.pallas_call(kernel, out_shape=jax.ShapeDtypeStruct((2, width, BLOCK),...  58.1 us
    transpose x1, local copies, waits for them, and re-layouts, body(): return turned.transpose(0, 2, 1).reshape(rows, width)  1.79 us

profile of v3, /device:TPU:30, one launch (start us, length us, event | category | flops | bytes accessed | tf_op | source)
XLA Modules:
  0.0 59.9 jit_solution(2756330983651415125)
XLA Ops:
  0.0 58.1 %shard_map.46 = bf16[2,128,512]{2,1,0:T(8,128)(2,1)} custom-call(s32[64,64]{1,0:T(8,128)} %mask_hbm.1, bf16[2,512,128]{2,1,0:T(8,128)(2,1)} %bitcast.4, bf16[64,128]{1,0:T(8,128)(2,1)} %k_ref.1, bf16[64,128]{1,0:T(8,128)(2,1)} %v_ref.1), custom_call_target="tpu_custom_call" | custom-call | tf_op jit(solution)/shard_map/pallas_call | solution.py:471
  58.1 1.8 %copy.5 = bf16[2,512,128]{2,1,0:T(8,128)(2,1)} copy(bf16[2,512,128]{1,2,0:T(8,128)(2,1)} %bitcast.3) | data formatting | bytes 524288 | tf_op jit(solution)/shard_map/transpose | solution.py:516

commit v4 on v3

--- a/solution.py
+++ b/solution.py
@@ -20,7 +20,7 @@
 LAST = 7
 ROUNDS = 4
 MESSAGES = 6
-EARLY = 2
+EARLY = 3
 NEG_FILL = -1e30
 NO_CAP = 3e38
 EXP_SCALE = 1.4426950408889634 * HEAD_DIM**-0.5
@@ -55,6 +55,7 @@
     ssend,
     srecv,
     sin,
+    obuf,
     info_i,
     info_j,
     info_prev,
@@ -73,6 +74,7 @@
     sib_recv,
     o_sem,
     s_sem,
+    out_sem,
 ):
     r = lax.axis_index("row")
     c = lax.axis_index("col")
@@ -154,12 +156,12 @@
         for d in (1, 3):
             drain(pieces(first, count, lax.rem(y + RING - d, RING)), yb_recv.at[n, way, d // 2])
 
-    def shared(first, count, of_core):
-        return kv.at[pl.ds(HERE + first, count), :, of_core]
-
-    def share(n, way, first, count):
-        view = shared(first, count, core)
-        remote(view, view, sib_send, sib_recv.at[n, way], sibling).start()
+    def shared(first, count, of_core, of_parity):
+        return kv.at[pl.ds(HERE + first, count), of_parity, of_core]
+
+    def share(n, way, first, count, part):
+        view = shared(first, count, core, parity if part == 0 else 1 - parity)
+        remote(view, view, sib_send, sib_recv.at[n, way, part], sibling).start()
 
     def arrivals(n):
         if n == 0:
@@ -195,6 +197,7 @@
     for hop in (2, -2, 1, -1):
         send_z(3, 0, hop)
     spread(0, 0, 0, 1)
+    share(0, 0, 0, 1, 0)
 
     zh = c // RING
 
@@ -314,7 +317,8 @@
 
     def wait_shared(n):
         for way, first, count in arrivals(n):
-            drain(shared(first, count, 1 - core), sib_recv.at[n, way])
+            drain(shared(first, count, 1 - core, parity), sib_recv.at[n, way, 0])
+            drain(shared(first, count, 1 - core, 1 - parity), sib_recv.at[n, way, 1])
 
     for n in range(1, ROUNDS + 1):
         for hops in ((2, -2), (1, -1)):
@@ -331,9 +335,10 @@
                     for stream in range(4):
                         wait_z(stream, o)
             spread(n, way, first, count)
+            share(n, way, first, count, 0)
         for way, first, count in arrivals(n - 1):
             gathered(n - 1, way, first, count)
-            share(n - 1, way, first, count)
+            share(n - 1, way, first, count, 1)
         if n == 1:
             own_mask.wait()
             prepare()
@@ -349,7 +354,7 @@
     early(near0, 0, RING)
     for way, first, count in arrivals(ROUNDS):
         gathered(ROUNDS, way, first, count)
-        share(ROUNDS, way, first, count)
+        share(ROUNDS, way, first, count, 1)
     wait_shared(ROUNDS - 1)
     copy = bring(near1, 1)
     copy.start()
@@ -445,11 +450,24 @@
         return carry
 
     lax.fori_loop(0, RING, head_body, 0)
-    arrived(2, 3, 4, 5)
-    for i in (0, 1):
-        parts = [(osend[0, i], ssend[0, i]), (orecv[0, i], srecv[0, i]), (orecv[1, i], srecv[1, i])]
+    outs = []
+    for m, i in ((3, 0), (2, 1)):
+        arrived(m)
+        parts = [(osend[0, i], ssend[0, i]), (orecv[1 - i, i], srecv[1 - i, i])]
         values, shares, top, total = merged(parts)
-        o_ref[i] = sum(p * (a / total) for p, a in zip(values, shares)).astype(bf16)
+        state[0, i, :HEAD_DIM] = sum(p * a for p, a in zip(values, shares))
+        state[0, i, HEAD_DIM : HEAD_DIM + 1] = total
+        maxima[0, i] = top
+    for m, i in ((4, 0), (5, 1)):
+        arrived(m)
+        tops = [maxima[0, i], srecv[i, i, 0:1]]
+        top = jnp.maximum(*tops)
+        shares = [jnp.exp2((a - top) * EXP_SCALE) for a in tops]
+        total = state[0, i, HEAD_DIM : HEAD_DIM + 1] * shares[0] + srecv[i, i, 1:2] * shares[1]
+        shares = [a / total for a in shares]
+        obuf[i] = (state[0, i, :HEAD_DIM] * shares[0] + orecv[i, i].astype(f32) * shares[1]).astype(bf16)
+        outs.append(pltpu.make_async_copy(obuf.at[i], o_ref.at[i], out_sem.at[i]))
+        outs[i].start()
 
     for d in (1, 2, 3):
         q_copies[d - 1].wait_send()
@@ -462,17 +480,18 @@
     for stream in range(4):
         drain(kv.at[pl.ds(0, ZRING - 1), parity, core, 0, 0], z_send.at[stream])
     drain(kv.at[:, :, core], sib_send)
+    for copy in outs:
+        copy.wait()
 
 
 def body(queries, key_vectors, value_vectors, block_mask):
     rows, width = queries.shape
-    vmem = pl.BlockSpec(memory_space=pltpu.VMEM)
     dma = pltpu.SemaphoreType.DMA
     turned = pl.pallas_call(
         kernel,
         out_shape=jax.ShapeDtypeStruct((2, width, BLOCK), bf16),
         in_specs=[pl.BlockSpec(memory_space=pltpu.HBM)] * 4,
-        out_specs=vmem,
+        out_specs=pl.BlockSpec(memory_space=pltpu.HBM),
         scratch_shapes=[
             pltpu.SMEM(block_mask.shape, jnp.int32),
             pltpu.VMEM((RING, 2, BLOCK, HEAD_DIM), bf16),
@@ -490,6 +509,7 @@
             pltpu.VMEM((RING, 2, 8, BLOCK), f32),
             pltpu.VMEM((2, 2, 8, BLOCK), f32),
             pltpu.VMEM((2, 8, BLOCK), f32),
+            pltpu.VMEM((2, HEAD_DIM, BLOCK), bf16),
             pltpu.SMEM((NSLOT,), jnp.int32),
             pltpu.SMEM((NSLOT,), jnp.int32),
             pltpu.SMEM((NSLOT,), jnp.int32),
@@ -505,9 +525,10 @@
             dma((4,)),
             dma((4, ZRING)),
             dma,
-            dma((ROUNDS + 1, 2)),
+            dma((ROUNDS + 1, 2, 2)),
             dma((2, MESSAGES)),
             dma((2, MESSAGES)),
+            dma((2,)),
         ],
         compiler_params=pltpu.CompilerParams(
             collective_id=0, has_side_effects=True, vmem_limit_bytes=58 * 2**20

time: 60 us -> 59.3 us (0.988)
  Pallas kernels: 58.1 us -> 57.4 us
    pallas_call x1, Pallas kernels: 58.1 us -> 57.4 us  [body(): pl.pallas_call(kernel, out_shape=jax.ShapeDtypeStruct((2, width, BLOCK),...]
where the time goes in v4:
time: 59.3 us; the launch traced here: 59.2 us
  Pallas kernels  57.4 us (97%)
  local copies, waits for them, and re-layouts  1.79 us (3%)
    pallas_call x1, Pallas kernels, body(): pl.pallas_call(kernel, out_shape=jax.ShapeDtypeStruct((2, width, BLOCK),...  57.4 us
    transpose x1, local copies, waits for them, and re-layouts, body(): return turned.transpose(0, 2, 1).reshape(rows, width)  1.79 us

profile of v4, /device:TPU:30, one launch (start us, length us, event | category | flops | bytes accessed | tf_op | source)
XLA Modules:
  0.0 59.2 jit_solution(6101384937125860771)
XLA Ops:
  0.0 57.4 %shard_map.46 = bf16[2,128,512]{2,1,0:T(8,128)(2,1)} custom-call(s32[64,64]{1,0:T(8,128)} %mask_hbm.1, bf16[2,512,128]{2,1,0:T(8,128)(2,1)} %bitcast.4, bf16[64,128]{1,0:T(8,128)(2,1)} %k_ref.1, bf16[64,128]{1,0:T(8,128)(2,1)} %v_ref.1), custom_call_target="tpu_custom_call" | custom-call | tf_op jit(solution)/shard_map/pallas_call | solution.py:490
  57.4 1.8 %copy.5 = bf16[2,512,128]{2,1,0:T(8,128)(2,1)} copy(bf16[2,512,128]{1,2,0:T(8,128)(2,1)} %bitcast.3) | data formatting | bytes 524288 | tf_op jit(solution)/shard_map/transpose | solution.py:537

commit v5 on v4

--- a/solution.py
+++ b/solution.py
@@ -332,9 +332,14 @@
         for way, first, count in arrivals(n):
             for o in range(first, first + count):
                 if n == ROUNDS or abs(o) % 2:
-                    for stream in range(4):
-                        wait_z(stream, o)
+                    wait_z(0, o)
+                    wait_z(1, o)
             spread(n, way, first, count)
+        for way, first, count in arrivals(n):
+            for o in range(first, first + count):
+                if n == ROUNDS or abs(o) % 2:
+                    wait_z(2, o)
+                    wait_z(3, o)
             share(n, way, first, count, 0)
         for way, first, count in arrivals(n - 1):
             gathered(n - 1, way, first, count)

time: 59.3 us -> 58.6 us (0.988)
  Pallas kernels: 57.4 us -> 56.6 us
    pallas_call x1, Pallas kernels: 57.4 us -> 56.6 us  [body(): pl.pallas_call(kernel, out_shape=jax.ShapeDtypeStruct((2, width, BLOCK),...]
where the time goes in v5:
time: 58.6 us; the launch traced here: 58.4 us
  Pallas kernels  56.6 us (97%)
  local copies, waits for them, and re-layouts  1.79 us (3%)
    pallas_call x1, Pallas kernels, body(): pl.pallas_call(kernel, out_shape=jax.ShapeDtypeStruct((2, width, BLOCK),...  56.6 us
    transpose x1, local copies, waits for them, and re-layouts, body(): return turned.transpose(0, 2, 1).reshape(rows, width)  1.79 us

profile of v5, /device:TPU:30, one launch (start us, length us, event | category | flops | bytes accessed | tf_op | source)
XLA Modules:
  0.0 58.4 jit_solution(14114517724836191073)
XLA Ops:
  0.0 56.6 %shard_map.46 = bf16[2,128,512]{2,1,0:T(8,128)(2,1)} custom-call(s32[64,64]{1,0:T(8,128)} %mask_hbm.1, bf16[2,512,128]{2,1,0:T(8,128)(2,1)} %bitcast.4, bf16[64,128]{1,0:T(8,128)(2,1)} %k_ref.1, bf16[64,128]{1,0:T(8,128)(2,1)} %v_ref.1), custom_call_target="tpu_custom_call" | custom-call | tf_op jit(solution)/shard_map/pallas_call | solution.py:495
  56.6 1.8 %copy.5 = bf16[2,512,128]{2,1,0:T(8,128)(2,1)} copy(bf16[2,512,128]{1,2,0:T(8,128)(2,1)} %bitcast.3) | data formatting | bytes 524288 | tf_op jit(solution)/shard_map/transpose | solution.py:542
